TPU v7x, 32 devices: a whole 2x2x4 slice. The times are simulated.
32 devices in a mesh: req: 16 (over z, y, core), tok: 2 (over x).
Axes of the slice: x: 2, y: 2, z: 4, core: 2. Of those that a mesh axis runs over, the one named last changes fastest.
Arguments:
- hidden_in: bfloat16 [32, 256, 2560], P('req', 'tok'), may hold values from -40 to 40
- cache_keys: bfloat16 [32, 4096, 320], P('req', None, 'tok'), may hold values from -100 to 100
- stored_cache_values: bfloat16 [32, 4096, 320], P('req', None, 'tok'), may hold values from -5 to 5
- cache_lengths: int32 [32], P('req'), may hold values from 0 to 16384, as said below
- live_slots: int32 [32], replicated, may hold values from 0 to 1, as said below
- attn_gain: float32 [2560], replicated, may hold values from 0.1 to 1.9
- w_query: bfloat16 [2560, 1280], P(None, 'tok'), may hold values from -0.125 to 0.125
- key_weight: bfloat16 [2560, 320], P(None, 'tok'), may hold values from -0.125 to 0.125
- value_weight: bfloat16 [2560, 320], P(None, 'tok'), may hold values from -0.125 to 0.125
- w_out: bfloat16 [1280, 2560], P('tok'), may hold values from -0.15625 to 0.15625
- mlp_gain: float32 [2560], replicated, may hold values from 0.1 to 1.9
- w_gate: bfloat16 [2560, 3584], P(None, 'tok'), may hold values from -0.125 to 0.125
- w_up: bfloat16 [2560, 3584], P(None, 'tok'), may hold values from -0.125 to 0.125
- w_down: bfloat16 [3584, 2560], P('tok'), may hold values from -0.09375 to 0.09375
Outputs:
- hidden_out: bfloat16 [32, 256, 2560], P('req', 'tok')
- new_keys: bfloat16 [32, 256, 320], P('req', None, 'tok')
- new_values: bfloat16 [32, 256, 320], P('req', None, 'tok')
Inputs may be any that keep to these rules, and one draw needn't show every extreme that they name: `live_slots`: exactly 16 of the 32 slots are live; the 2 slots of one index of req hold 0, 1 or 2 live requests, and some index holds two. `cache_lengths`: 0 for a slot that is not live; some live slot has exactly 16384.
All inputs are finite; a program needn't handle non-finite values.
Results may differ from a plain program's by a relative error of at most 0.0095.
Values may be sent and summed in bfloat16 or wider, within the bound.
A program may use at most 192 MiB of HBM per device.

v0:
```python
import jax
import jax.numpy as jnp
from jax import lax
from jax.sharding import PartitionSpec as P

HEAD_DIM = 80


EPSILON = 1e-05
ROPE_BASE = 10000.0


def rms_norm(values, norm_gain):
    widened = values.astype(jnp.float32)
    mean_square = jnp.mean(widened * widened, axis=-1, keepdims=True)
    return widened * lax.rsqrt(mean_square + EPSILON) * norm_gain


def apply_rotary(values, token_positions):
    full_width = values.shape[-1]
    half_width = full_width // 2
    inverse = ROPE_BASE ** (-(jnp.arange(half_width, dtype=jnp.float32) * 2.0) / full_width)
    angles = token_positions.astype(jnp.float32)[..., None] * inverse
    cosine = jnp.cos(angles)[..., None, :]
    sine_part = jnp.sin(angles)[..., None, :]
    first_half = values[..., :half_width]
    second_half = values[..., half_width:]
    return jnp.concatenate(
        [
            first_half * cosine - second_half * sine_part,
            second_half * cosine + first_half * sine_part,
        ],
        axis=-1,
    )


def attend(
    query_rows, cached_keys, cached_values, recent_keys, recent_values, length, query_group_count
):
    row_total = query_rows.shape[0]
    recent_count = recent_keys.shape[0]
    window = cached_keys.shape[0]
    block_size = min(512, window)
    block_count = window // block_size
    scaling = query_rows.shape[1] ** (-0.5)
    query_pos = length + jnp.arange(row_total, dtype=jnp.int32) // query_group_count

    def cache_scores(block_index):
        key_block = lax.dynamic_slice_in_dim(cached_keys, block_index * block_size, block_size, 0)
        scores = (
            jnp.einsum("rd,kd->rk", query_rows, key_block, preferred_element_type=jnp.float32)
            * scaling
        )
        key_pos = (
            length - window + block_index * block_size + jnp.arange(block_size, dtype=jnp.int32)
        )
        visible = (key_pos[None, :] >= 0) & (query_pos[:, None] - key_pos[None, :] < window)
        return jnp.where(visible, scores, -jnp.inf)

    recent_pos = length + jnp.arange(recent_count, dtype=jnp.int32)
    recent_scores = (
        jnp.einsum("rd,kd->rk", query_rows, recent_keys, preferred_element_type=jnp.float32)
        * scaling
    )
    recent_visible = (recent_pos[None, :] <= query_pos[:, None]) & (
        query_pos[:, None] - recent_pos[None, :] < window
    )
    recent_scores = jnp.where(recent_visible, recent_scores, -jnp.inf)
    start_top = jnp.max(recent_scores, axis=1, keepdims=True)
    start_mass = jnp.sum(jnp.exp(recent_scores - start_top), axis=1, keepdims=True)
    first_block = jnp.maximum(window - length, 0) // block_size
    score_store = jnp.full((block_count, row_total, block_size), -jnp.inf, jnp.float32)

    def add_stats(block_index, carry):
        top, mass, stored = carry
        scores = cache_scores(block_index)
        stored = lax.dynamic_update_index_in_dim(stored, scores, block_index, 0)
        raised = jnp.maximum(top, jnp.max(scores, axis=1, keepdims=True))
        mass = mass * jnp.exp(top - raised) + jnp.sum(
            jnp.exp(scores - raised), axis=1, keepdims=True
        )
        return (raised, mass, stored)

    top, mass, score_store = lax.fori_loop(
        first_block, block_count, add_stats, (start_top, start_mass, score_store)
    )

    def weights(scores):
        return (jnp.exp(scores - top) / mass).astype(jnp.bfloat16)

    start_sum = jnp.dot(weights(recent_scores), recent_values, preferred_element_type=jnp.float32)

    def add_values(block_index, running):
        value_block = lax.dynamic_slice_in_dim(
            cached_values, block_index * block_size, block_size, 0
        )
        scores = lax.dynamic_index_in_dim(score_store, block_index, 0, keepdims=False)
        return running + jnp.dot(weights(scores), value_block, preferred_element_type=jnp.float32)

    return lax.fori_loop(first_block, block_count, add_values, start_sum)


def feed_forward(rows_in, mlp_gain, w_gate, w_up, w_down):
    normed_rows = rms_norm(rows_in, mlp_gain).astype(jnp.bfloat16)
    block_rows = lax.all_gather(normed_rows, "tok", axis=0, tiled=True)
    gate_part = jnp.dot(block_rows, w_gate, preferred_element_type=jnp.float32)
    up_part = jnp.dot(block_rows, w_up, preferred_element_type=jnp.float32)
    activated = (jax.nn.silu(gate_part) * up_part).astype(jnp.bfloat16)
    summed = lax.psum_scatter(
        jnp.dot(
            lax.slice_in_dim(activated, 0, rows_in.shape[0] * lax.axis_size("tok"), axis=0),
            w_down,
            preferred_element_type=jnp.float32,
        ).astype(jnp.bfloat16),
        "tok",
        scatter_dimension=0,
        tiled=True,
    ).astype(jnp.float32)
    return (rows_in.astype(jnp.float32) + summed).astype(jnp.bfloat16)


def local(
    hidden_in,
    cache_keys,
    stored_cache_values,
    cache_lengths,
    live_slots,
    attn_gain,
    w_query,
    key_weight,
    value_weight,
    w_out,
    mlp_gain,
    w_gate,
    w_up,
    w_down,
):
    slots, quarter, model_width = hidden_in.shape
    new_rows = quarter * lax.axis_size("tok")
    query_width = w_query.shape[1]
    key_width = key_weight.shape[1]
    query_heads = query_width // HEAD_DIM
    key_heads = key_width // HEAD_DIM
    query_group_count = query_heads // key_heads
    alive_slots = lax.dynamic_slice_in_dim(live_slots, lax.axis_index("req") * slots, slots)
    window_mask = alive_slots[:, None, None] > 0
    empty_value_rows = jnp.zeros((), jnp.bfloat16)
    normed = rms_norm(hidden_in, attn_gain).astype(jnp.bfloat16)
    block_rows = lax.all_gather(normed, "tok", axis=1, tiled=True)
    mixed_rows = jnp.concatenate(
        [
            jnp.einsum("srd,dh->srh", block_rows, matrix, preferred_element_type=jnp.float32)
            for matrix in (w_query, key_weight, value_weight)
        ],
        axis=2,
    )
    token_positions = cache_lengths[:, None] + jnp.arange(new_rows, dtype=jnp.int32)[None, :]
    queries = apply_rotary(
        mixed_rows[..., :query_width].reshape(slots, new_rows, query_heads, HEAD_DIM),
        token_positions,
    ).astype(jnp.bfloat16)
    incoming_keys = apply_rotary(
        mixed_rows[..., query_width : query_width + key_width].reshape(
            slots, new_rows, key_heads, HEAD_DIM
        ),
        token_positions,
    ).astype(jnp.bfloat16)
    incoming_values = (
        mixed_rows[..., query_width + key_width :]
        .astype(jnp.bfloat16)
        .reshape(slots, new_rows, key_heads, HEAD_DIM)
    )
    new_keys = jnp.where(
        window_mask, incoming_keys.reshape(slots, new_rows, key_width), empty_value_rows
    )
    new_values = jnp.where(
        window_mask, incoming_values.reshape(slots, new_rows, key_width), empty_value_rows
    )
    slot_results = []
    for slot_index in range(slots):
        head_results = []
        for current_head_index in range(key_heads):
            query_rows = queries[
                slot_index,
                :,
                current_head_index
                * query_group_count : (current_head_index + 1)
                * query_group_count,
                :,
            ].reshape(new_rows * query_group_count, HEAD_DIM)
            final_output = attend(
                query_rows,
                cache_keys[
                    slot_index,
                    :,
                    current_head_index * HEAD_DIM : (current_head_index + 1) * HEAD_DIM,
                ],
                stored_cache_values[
                    slot_index,
                    :,
                    current_head_index * HEAD_DIM : (current_head_index + 1) * HEAD_DIM,
                ],
                incoming_keys[slot_index, :, current_head_index, :],
                incoming_values[slot_index, :, current_head_index, :],
                cache_lengths[slot_index],
                query_group_count,
            )
            head_results.append(final_output.reshape(new_rows, query_group_count * HEAD_DIM))
        slot_results.append(jnp.concatenate(head_results, axis=1))
    attended = jnp.stack(slot_results, axis=0).astype(jnp.bfloat16)
    block_rows = attended
    projected = lax.psum_scatter(
        jnp.einsum("sth,hd->tsd", block_rows, w_out, preferred_element_type=jnp.float32).astype(
            jnp.bfloat16
        ),
        "tok",
        scatter_dimension=0,
        tiled=True,
    ).astype(jnp.float32)
    projected = jnp.transpose(projected, (1, 0, 2))
    residual = (hidden_in.astype(jnp.float32) + projected).astype(jnp.bfloat16)
    spread_rows = lax.all_to_all(residual, "req", split_axis=1, concat_axis=0, tiled=True)
    picked_index = jnp.nonzero(live_slots > 0, size=lax.axis_size("req"), fill_value=0)[0].astype(
        jnp.int32
    )
    picked = jnp.take(spread_rows, picked_index, axis=0)
    completed_output = feed_forward(
        picked.reshape(-1, model_width), mlp_gain, w_gate, w_up, w_down
    ).reshape(picked.shape)
    placed = jnp.zeros_like(spread_rows).at[picked_index].set(completed_output)
    hidden_out = lax.all_to_all(placed, "req", split_axis=0, concat_axis=1, tiled=True)
    return (hidden_out, new_keys, new_values)


def solution(mesh):
    return jax.shard_map(
        local,
        mesh=mesh,
        in_specs=(
            P("req", "tok", None),
            P("req", None, "tok"),
            P("req", None, "tok"),
            P("req"),
            P(),
            P(),
            P(None, "tok"),
            P(None, "tok"),
            P(None, "tok"),
            P("tok", None),
            P(),
            P(None, "tok"),
            P(None, "tok"),
            P("tok", None),
        ),
        out_specs=(P("req", "tok", None), P("req", None, "tok"), P("req", None, "tok")),
        check_vma=False,
    )
```

profile of v0, /device:TPU:1, one launch (start us, length us, event | category | flops | bytes accessed | tf_op | source)
XLA Modules:
  0.0 775.9 jit_solution(13139277975490981411)
XLA Ops:
  20.2 3.5 fusion.113
  43.8 8.7 %all-gather.3.cloned.1.call-done = bf16[2,256,2560]{2,1,0:T(8,128)(2,1)} async-done(((bf16[2,128,2560]{2,1,0:T(8,128)(2,1)}), bf16[2,256,2560]{2,1,0:T(8,128)(2,1)}) %all-gather.3.cloned.1.call-update) | async-done | bytes 2621456 | tf_op jit(solution)/shard_map/all_gather | solution.py:149
  52.5 4.6 fusion.62
  64.6 7.9 %broadcast.468.clone.3 = f32[8,1024,512]{1,2,0:T(8,128)} broadcast(f32[]{:T(128)} %constant.371.clone.1), dimensions={} | broadcast | bytes 16777220 | tf_op jit(solution)/shard_map/broadcast.53
  72.5 59.0 %while.114 = (s32[]{:T(128)}, f32[1024,1]{0,1:T(1,128)S(1)}, f32[1024,1]{0,1:T(1,128)S(1)}, f32[8,1024,512]{1,2,0:T(8,128)}, s32[]{:T(128)}, /*index=5*/bf16[409...) while((s32[]{:T(128)}, f32[1024,1]{0,1:T(1,128)S(1)}, ...), condition=%wide.region_26.27_spmd.clone, body=%wide.region_23.26_spmd.clone.sunk | while | flops 88093192 | bytes 17138952 | solution.py:84
  76.1 3.3 bitcast_dynamic-update-slice_fusion.10
  90.9 3.3 bitcast_dynamic-update-slice_fusion.10
  98.2 3.3 bitcast_dynamic-update-slice_fusion.10
  105.6 3.4 bitcast_dynamic-update-slice_fusion.10
  113.1 3.3 bitcast_dynamic-update-slice_fusion.10
  120.4 3.3 bitcast_dynamic-update-slice_fusion.10
  127.8 3.3 bitcast_dynamic-update-slice_fusion.10
  131.5 3.7 broadcast_select_fusion
  136.3 74.0 %while.110 = (s32[]{:T(128)}, f32[1024,80]{0,1:T(8,128)}, f32[8,1024,512]{1,2,0:T(8,128)}, f32[1024,1]{0,1:T(1,128)S(1)}, f32[1024,1]{0,1:T(1,128)S(1)}, /*index...) while((s32[]{:T(128)}, f32[1024,80]{0,1:T(8,128)}, ...), condition=%wide.region_28.29_spmd, body=%wide.region_27.28_spmd.sunk | while | flops 85540872 | bytes 11280581 | solution.py:100
  217.4 7.9 %broadcast.468.clone.2 = f32[8,1024,512]{1,2,0:T(8,128)} broadcast(f32[]{:T(128)} %constant.371.clone.1), dimensions={} | broadcast | bytes 16777220 | tf_op jit(solution)/shard_map/broadcast.53
  225.3 59.3 %while.115 = (s32[]{:T(128)}, f32[1024,1]{0,1:T(1,128)S(1)}, f32[1024,1]{0,1:T(1,128)S(1)}, f32[8,1024,512]{1,2,0:T(8,128)}, s32[]{:T(128)}, /*index=5*/bf16[409...) while((s32[]{:T(128)}, f32[1024,1]{0,1:T(1,128)S(1)}, ...), condition=%wide.region_34.35_spmd.clone, body=%wide.region_31.34_spmd.clone.sunk | while | flops 88093192 | bytes 17138952 | solution.py:84
  228.9 3.3 bitcast_dynamic-update-slice_fusion.11
  243.7 3.3 bitcast_dynamic-update-slice_fusion.11
  251.2 3.3 bitcast_dynamic-update-slice_fusion.11
  258.6 3.4 bitcast_dynamic-update-slice_fusion.11
  266.1 3.3 bitcast_dynamic-update-slice_fusion.11
  273.4 3.3 bitcast_dynamic-update-slice_fusion.11
  280.9 3.3 bitcast_dynamic-update-slice_fusion.11
  286.9 73.8 %while.111 = (s32[]{:T(128)}, f32[1024,80]{0,1:T(8,128)}, f32[8,1024,512]{1,2,0:T(8,128)}, f32[1024,1]{0,1:T(1,128)S(1)}, f32[1024,1]{0,1:T(1,128)S(1)}, /*index...) while((s32[]{:T(128)}, f32[1024,80]{0,1:T(8,128)}, ...), condition=%wide.region_36.37_spmd, body=%wide.region_35.36_spmd.sunk | while | flops 85540872 | bytes 11280581 | solution.py:100
  367.8 7.9 %broadcast.468.clone.1 = f32[8,1024,512]{1,2,0:T(8,128)} broadcast(f32[]{:T(128)} %constant.371.clone.1), dimensions={} | broadcast | bytes 16777220 | tf_op jit(solution)/shard_map/broadcast.53
  375.6 37.1 %while.112 = (s32[]{:T(128)}, f32[1024,1]{0,1:T(1,128)S(1)}, f32[1024,1]{0,1:T(1,128)S(1)}, f32[8,1024,512]{1,2,0:T(8,128)}, s32[]{:T(128)}, /*index=5*/bf16[409...) while((s32[]{:T(128)}, f32[1024,1]{0,1:T(1,128)S(1)}, ...), condition=%wide.region_10.11_spmd.clone, body=%wide.region_7.10_spmd.clone.sunk | while | flops 88093192 | bytes 17138952 | solution.py:84
  379.3 3.3 bitcast_dynamic-update-slice_fusion.8
  386.7 3.4 bitcast_dynamic-update-slice_fusion.8
  401.6 3.3 bitcast_dynamic-update-slice_fusion.8
  409.0 3.3 bitcast_dynamic-update-slice_fusion.8
  415.0 46.1 %while.108 = (s32[]{:T(128)}, f32[1024,80]{0,1:T(8,128)}, f32[8,1024,512]{1,2,0:T(8,128)}, f32[1024,1]{0,1:T(1,128)S(1)}, f32[1024,1]{0,1:T(1,128)S(1)}, /*index...) while((s32[]{:T(128)}, f32[1024,80]{0,1:T(8,128)}, ...), condition=%wide.region_12.13_spmd, body=%wide.region_11.12_spmd.sunk | while | flops 85540872 | bytes 11280581 | solution.py:100
  468.2 7.9 %broadcast.468.clone = f32[8,1024,512]{1,2,0:T(8,128)} broadcast(f32[]{:T(128)} %constant.371.clone.1), dimensions={} | broadcast | bytes 16777220 | tf_op jit(solution)/shard_map/broadcast.53
  476.1 37.3 %while.113 = (s32[]{:T(128)}, f32[1024,1]{0,1:T(1,128)S(1)}, f32[1024,1]{0,1:T(1,128)S(1)}, f32[8,1024,512]{1,2,0:T(8,128)}, s32[]{:T(128)}, /*index=5*/bf16[409...) while((s32[]{:T(128)}, f32[1024,1]{0,1:T(1,128)S(1)}, ...), condition=%wide.region_18.19_spmd.clone, body=%wide.region_15.18_spmd.clone.sunk | while | flops 88093192 | bytes 17138952 | solution.py:84
  480.0 3.3 bitcast_dynamic-update-slice_fusion.9
  487.4 3.4 bitcast_dynamic-update-slice_fusion.9
  494.9 3.3 bitcast_dynamic-update-slice_fusion.9
  502.3 3.3 bitcast_dynamic-update-slice_fusion.9
  509.7 3.3 bitcast_dynamic-update-slice_fusion.9
  515.7 46.1 %while.109 = (s32[]{:T(128)}, f32[1024,80]{0,1:T(8,128)}, f32[8,1024,512]{1,2,0:T(8,128)}, f32[1024,1]{0,1:T(1,128)S(1)}, f32[1024,1]{0,1:T(1,128)S(1)}, /*index...) while((s32[]{:T(128)}, f32[1024,80]{0,1:T(8,128)}, ...), condition=%wide.region_20.21_spmd, body=%wide.region_19.20_spmd.sunk | while | flops 85540872 | bytes 11280581 | solution.py:100
  566.9 3.7 fusion.60
  570.6 33.5 %reduce-scatter.3.cloned.1.call-done = bf16[128,2,2560]{2,0,1:T(8,128)(2,1)} async-done(((bf16[256,2,2560]{2,0,1:T(8,128)(2,1)}), bf16[128,2,2560]{2,0,1:T(8,128)(2,1)}) %reduce-scatter.3.cloned.1.call-update) | async-done | bytes 1310736 | tf_op jit(solution)/shard_map/reduce_scatter | solution.py:212
  608.5 6.2 all-to-all-start
  618.2 24.4 %all-to-all-done = bf16[2,128,2560]{2,0,1:T(2,128)(2,1)} async-done(((bf16[2,128,2560]{2,0,1:T(2,128)(2,1)}), bf16[2,128,2560]{2,0,1:T(2,128)(2,1)}, u32[]{:S(2)}, u32[]{:S(2)}) %all-to-all-start) | async-done | bytes 1310752 | tf_op jit(solution)/shard_map/all_to_all | solution.py:222
  652.8 25.6 %all-gather.5.cloned.1.call-done = bf16[256,2560]{1,0:T(8,128)(2,1)} async-done(((bf16[128,2560]{1,0:T(8,128)(2,1)}), bf16[256,2560]{1,0:T(8,128)(2,1)}) %all-gather.5.cloned.1.call-update) | async-done | bytes 1310736 | tf_op jit(solution)/shard_map/all_gather | solution.py:105
  678.3 7.8 %fusion.120 = f32[256,1792]{1,0:T(8,128)} fusion(bf16[256,2560]{1,0:T(8,128)(2,1)} %all-gather.5.cloned.1.call-done, bf16[2560,1792]{1,0:T(8,128)(2,1)} %param.41), kind=kOutput, calls=%fused_computation.249 | convolution fusion | flops 2348810240 | bytes 12320768 | tf_op jit(solution)/shard_map/dot_general | solution.py:106
  686.1 13.7 %convolution_convert_fusion.1 = bf16[256,2560]{1,0:T(8,128)(2,1)} fusion(bf16[1792,2560]{1,0:T(8,128)(2,1)} %param.43, bf16[256,2560]{1,0:T(8,128)(2,1)} %all-gather.5.cloned.1.call-done, bf16[2560,1792]{1,0:T(8,128)(2,1)} %param.42, f32[256,1792]{1,0:T(8,128)} %fusion.120), kind=kOutput, calls=%fused_computation.116 | convolution fusion | flops 4701028352 | bytes 22806528 | tf_op jit(solution)/shard_map/dot_general | solution.py:110
  699.8 23.3 %reduce-scatter.5.cloned.1.call-done = bf16[128,2560]{1,0:T(8,128)(2,1)} async-done(((bf16[256,2560]{1,0:T(8,128)(2,1)}), bf16[128,2560]{1,0:T(8,128)(2,1)}) %reduce-scatter.5.cloned.1.call-update) | async-done | bytes 655376 | tf_op jit(solution)/shard_map/reduce_scatter | solution.py:109
  729.7 38.1 %all_to_all.36 = bf16[32,8,2560]{2,1,0:T(8,128)(2,1)S(1)} all-to-all(bf16[32,8,2560]{2,1,0:T(8,128)(2,1)} %scatter_fusion), channel_id=1, replica_groups=mesh['req'=16,'tok'=2] {'req'}, dimensions={0} | all-to-all | bytes 2621440 | tf_op jit(solution)/shard_map/all_to_all | solution.py:231
  (471 shorter events, 451.6 us)
Async XLA Ops:
  7.2 559.7 %copy-start = (bf16[640,2560]{1,0:T(8,128)(2,1)S(1)}, bf16[640,2560]{1,0:T(8,128)(2,1)}, u32[]{:S(2)}) copy-start(bf16[640,2560]{1,0:T(8,128)(2,1)} %param.39) | copy-start | bytes 9830404
  7.2 45.3 %all-gather.3.cloned.1.call-start = ((), (), s32[]{:S(2)}) async-start(), calls=%async_computation.4 | async-start | bytes 3932160 | tf_op jit(solution)/shard_map/all_gather | solution.py:149
  7.2 1.9 copy-start.5
  9.1 2.3 copy-start.15
  11.2 592.8 %reduce-scatter.3.cloned.1.call-start = ((), (), s32[]{:S(2)}) async-start(), calls=%async_computation.5 | async-start | bytes 3932160 | tf_op jit(solution)/shard_map/reduce_scatter | solution.py:212
  34.9 4.5 copy-start.18
  40.7 22.3 %copy-start.23 = (s32[256]{0:T(256)}, s32[256]{0:T(256)S(1)}, u32[]{:S(2)}) copy-start(s32[256]{0:T(256)S(1)} %iota_add_fusion.4) | copy-start | bytes 3076
  42.6 20.4 %copy-start.16 = (s32[1024]{0:T(1024)}, s32[1024]{0:T(1024)S(1)}, u32[]{:S(2)}) copy-start(s32[1024]{0:T(1024)S(1)} %fusion.98) | copy-start | bytes 12292
  60.0 3.1 copy-start.11
  63.0 1.6 copy-start.13
  63.5 1.0 copy-start.7
  64.6 7.9 %copy-start.12 = (bf16[1,256,4,80]{3,2,1,0:T(4,128)(2,1)S(1)}, bf16[1,256,4,80]{3,2,1,0:T(4,128)(2,1)}, u32[]{:S(2)}) copy-start(bf16[1,256,4,80]{3,2,1,0:T(4,128)(2,1)} %copy.120) | copy-start | bytes 491524
  76.1 3.4 copy-start.1
  83.5 3.3 copy-start.1
  90.9 3.3 copy-start.1
  98.2 3.3 copy-start.1
  105.6 3.4 copy-start.1
  113.1 3.3 copy-start.1
  120.4 3.4 copy-start.1
  127.8 3.3 copy-start.1
  131.5 3.8 copy-start.8
  135.3 1.1 copy-start.20
  136.3 78.7 %copy-start.17 = (s32[1024]{0:T(1024)S(1)}, s32[1024]{0:T(1024)}, u32[]{:S(2)}) copy-start(s32[1024]{0:T(1024)} %copy-done.16) | copy-start | bytes 12292
  228.9 3.4 copy-start.2
  236.4 3.3 copy-start.2
  243.7 3.3 copy-start.2
  251.2 3.3 copy-start.2
  258.6 3.4 copy-start.2
  266.1 3.3 copy-start.2
  273.4 3.4 copy-start.2
  280.9 3.3 copy-start.2
  286.9 78.5 %copy-start.21 = (s32[256]{0:T(256)S(1)}, s32[256]{0:T(256)}, u32[]{:S(2)}) copy-start(s32[256]{0:T(256)} %iota_add_fusion.5) | copy-start | bytes 3076
  379.3 3.3 copy-start.3
  386.7 3.4 copy-start.3
  394.2 3.3 copy-start.3
  401.6 3.4 copy-start.3
  409.0 3.3 copy-start.3
  415.0 50.8 %copy-start.22 = (s32[256]{0:T(256)S(1)}, s32[256]{0:T(256)}, u32[]{:S(2)}) copy-start(s32[256]{0:T(256)} %iota_add_fusion.5) | copy-start | bytes 3076
  480.0 3.3 copy-start.4
  487.4 3.4 copy-start.4
  494.9 3.3 copy-start.4
  502.3 3.4 copy-start.4
  509.7 3.3 copy-start.4
  606.1 8.7 %copy-start.19 = (s32[32]{0:T(128)S(1)}, s32[32]{0:T(128)}, u32[]{:S(2)}) copy-start(s32[32]{0:T(128)} %param.34) | copy-start | bytes 388
  608.5 34.1 %all-to-all-start = ((bf16[2,128,2560]{2,0,1:T(2,128)(2,1)}), bf16[2,128,2560]{2,0,1:T(2,128)(2,1)}, u32[]{:S(2)}, u32[]{:S(2)}) async-start(bf16[2,128,2560]{2,0,1:T(2,128)(2,1)} %copy.130), calls=%async_computation.1 | async-start | bytes 2621440 | tf_op jit(solution)/shard_map/all_to_all | solution.py:222
  614.7 63.6 %all-gather.5.cloned.1.call-start = ((), (), s32[]{:S(2)}) async-start(), calls=%async_computation.6 | async-start | bytes 1966080 | tf_op jit(solution)/shard_map/all_gather | solution.py:105
  644.1 5.4 copy-start.14
  652.5 70.7 %reduce-scatter.5.cloned.1.call-start = ((), (), s32[]{:S(2)}) async-start(), calls=%async_computation.7 | async-start | bytes 1966080 | tf_op jit(solution)/shard_map/reduce_scatter | solution.py:109
  (3 other events, 2.9 us)
Sparse Core Ops, SparseCore 0:
  11.4 41.0 all-gather.2
  570.7 33.2 reduce-scatter.2
  652.6 25.7 all-gather.4
  700.0 23.1 reduce-scatter.4
where the time goes:
time: 789 us; the launch traced here: 776 us
  local copies, waits for them, and re-layouts  332 us (42%)
  matrix products  207 us (26%)
  waiting for transfers between devices  116 us (15%)
  other arithmetic  57.6 us (7%)
  blocking collectives  38.1 us (5%)
  between operations  17.5 us (2%)
    dynamic_slice x52, local copies, waits for them, and re-layouts, add_values(): lax.dynamic_index_in_dim(score_store, block_index, 0, keepdims=False)  158 us
    dynamic_update_slice x26, local copies, waits for them, and re-layouts, add_stats(): stored = lax.dynamic_update_index_in_dim(stored, scores, block_index, 0)  86.6 us
    dot_general x26, matrix products, add_values(): jnp.dot(weights(scores), value_block, preferred_element_type=jnp.float32)  81.7 us
    dot_general x26, matrix products, cache_scores(): jnp.einsum('rd,kd->rk', query_rows, key_block, preferred_element_type=jnp...  76.7 us
    all_to_all x1, blocking collectives, local(): lax.all_to_all(placed, 'req', split_axis=0, concat_axis=1, tiled=True)  38.1 us
    another operation x9, local copies, waits for them, and re-layouts  35.9 us
    reduce_scatter x1, waiting for transfers between devices, local(): lax.psum_scatter(jnp.einsum('sth,hd->tsd', block_rows, w_out, preferred_e...  33.5 us
    all_gather x1, waiting for transfers between devices, feed_forward(): block_rows = lax.all_gather(normed_rows, 'tok', axis=0, tiled=True)  25.6 us
  transfers between devices with their start and end apart: 5, of which 5 were waited for; matrix products, arithmetic and copies ran while one was open for 4% of the time, Pallas kernels for 0%

commit v1 on v0

v1 whole, which is shorter than its diff:
```python
import functools

import jax
import jax.numpy as jnp
from jax import lax
from jax.experimental import pallas as pl
from jax.experimental.pallas import tpu as pltpu
from jax.sharding import PartitionSpec as P

HEAD_DIM = 80
EPSILON = 1e-05
ROPE_BASE = 10000.0
LOG2E = 1.4426950408889634
KEY_BLOCK = 512
NT = (((1,), (1,)), ((), ()))


def attention_kernel(
    kv_heads,
    group,
    scal_ref,
    own_ref,
    other_ref,
    gain_ref,
    wq_ref,
    wk_ref,
    wv_ref,
    cos_ref,
    sin_ref,
    k_ref,
    v_ref,
    att_ref,
    nk_ref,
    nv_ref,
    nrm,
    q_s,
    kf_s,
    kpad,
    v_s,
    acc,
    top,
):
    heads = kv_heads * group
    half = own_ref.shape[0]
    rows = 2 * half
    window = k_ref.shape[0]
    kw = kv_heads * HEAD_DIM
    wide = acc.shape[2]
    qw = heads * HEAD_DIM
    length = scal_ref[0]
    alive = scal_ref[1]
    tok = scal_ref[2]
    scale = (HEAD_DIM**-0.5) * LOG2E

    @pl.when(alive == 0)
    def _():
        att_ref[...] = jnp.zeros_like(att_ref)
        nk_ref[...] = jnp.zeros_like(nk_ref)
        nv_ref[...] = jnp.zeros_like(nv_ref)

    @pl.when(alive > 0)
    def _():
        for part, ref in enumerate((own_ref, other_ref)):
            x = ref[...].astype(jnp.float32)
            ms = jnp.mean(x * x, axis=1, keepdims=True)
            nrm[part * half : (part + 1) * half, :] = (
                x * lax.rsqrt(ms + EPSILON) * gain_ref[...]
            ).astype(jnp.bfloat16)
        normed = nrm[...]
        x = jnp.dot(normed, wq_ref[...], preferred_element_type=jnp.float32)
        lane = lax.broadcasted_iota(jnp.int32, (rows, qw), 1)
        first = lax.rem(lane, HEAD_DIM) < HEAD_DIM // 2
        turned = jnp.where(
            first, pltpu.roll(x, qw - HEAD_DIM // 2, 1), pltpu.roll(x, HEAD_DIM // 2, 1)
        )
        q = x * cos_ref[...] + turned * sin_ref[...]
        lane2 = lax.broadcasted_iota(jnp.int32, (rows, wide), 1)
        for h in range(heads):
            g = h // group
            shift = (g * HEAD_DIM - h * HEAD_DIM) % qw
            r = q if shift == 0 else pltpu.roll(q, shift, 1)
            r = r[:, :wide]
            keep = (lane2 >= g * HEAD_DIM) & (lane2 < (g + 1) * HEAD_DIM)
            q_s[h] = jnp.where(keep, r, 0.0).astype(jnp.bfloat16)[:, :kw]
        kpad[...] = jnp.zeros_like(kpad)
        kpad[:, :kw] = jnp.dot(normed, wk_ref[...], preferred_element_type=jnp.float32)
        x = kpad[...]
        turned = jnp.where(
            lax.rem(lane2, HEAD_DIM) < HEAD_DIM // 2,
            pltpu.roll(x, wide - HEAD_DIM // 2, 1),
            pltpu.roll(x, HEAD_DIM // 2, 1),
        )
        fresh_k = (x * cos_ref[:, :wide] + turned * sin_ref[:, :wide]).astype(jnp.bfloat16)[:, :kw]
        kf_s[...] = fresh_k
        fresh_v = jnp.dot(normed, wv_ref[...], preferred_element_type=jnp.float32).astype(
            jnp.bfloat16
        )
        v_s[...] = jnp.ones_like(v_s)
        v_s[:window, :kw] = v_ref[...]
        v_s[window:, :kw] = fresh_v
        for part in range(2):
            start = pl.multiple_of((tok if part == 0 else 1 - tok) * half, half)
            nk_ref[pl.ds(start, half), :] = fresh_k[part * half : (part + 1) * half]
            nv_ref[pl.ds(start, half), :] = fresh_v[part * half : (part + 1) * half]

        def token_of(index):
            return index + jnp.where(index < half, tok * half, -tok * half)

        row_t = token_of(lax.broadcasted_iota(jnp.int32, (rows, rows), 0))
        col_t = token_of(lax.broadcasted_iota(jnp.int32, (rows, rows), 1))
        seen = col_t <= row_t
        keys = kf_s[...]
        vals = v_s[window:, :]
        for h in range(heads):
            s = lax.dot_general(q_s[h], keys, NT, preferred_element_type=jnp.float32) * scale
            s = jnp.where(seen, s, -jnp.inf)
            m = jnp.broadcast_to(jnp.max(s, axis=1, keepdims=True), (rows, 128))
            p = jnp.exp2(s - jnp.concatenate([m] * (rows // 128), axis=1))
            top[h] = m
            acc[h] = jnp.dot(p.astype(jnp.bfloat16), vals, preferred_element_type=jnp.float32)

        def block(index, masked):
            start = pl.multiple_of(index * KEY_BLOCK, KEY_BLOCK)
            keys = k_ref[pl.ds(start, KEY_BLOCK), :]
            vals = v_s[pl.ds(start, KEY_BLOCK), :]
            if masked:
                row_t = token_of(lax.broadcasted_iota(jnp.int32, (rows, KEY_BLOCK), 0))
                col = start + lax.broadcasted_iota(jnp.int32, (rows, KEY_BLOCK), 1)
                seen = (col > row_t) & (col >= window - length)
            for h in range(heads):
                s = lax.dot_general(q_s[h], keys, NT, preferred_element_type=jnp.float32) * scale
                if masked:
                    s = jnp.where(seen, s, -jnp.inf)
                old = top[h]
                m = jnp.maximum(old, jnp.max(s, axis=1, keepdims=True))
                p = jnp.exp2(s - jnp.concatenate([m] * (KEY_BLOCK // 128), axis=1))
                alpha = jnp.exp2(old - m)
                top[h] = m
                acc[h] = acc[h] * jnp.concatenate([alpha] * (wide // 128), axis=1) + jnp.dot(
                    p.astype(jnp.bfloat16), vals, preferred_element_type=jnp.float32
                )

        blocks = window // KEY_BLOCK
        first_block = jnp.maximum(window - length, 0) // KEY_BLOCK

        @pl.when(first_block < blocks)
        def _():
            block(first_block, True)

        @pl.loop(first_block + 1, blocks)
        def _(index):
            block(index, False)

        total = jnp.zeros((rows, qw), jnp.float32)
        for h in range(heads):
            g = h // group
            a = acc[h]
            o = a / a[:, kw : kw + 1]
            keep = (lane2 >= g * HEAD_DIM) & (lane2 < (g + 1) * HEAD_DIM)
            o = jnp.where(keep, o, 0.0)
            o = jnp.concatenate([o, jnp.zeros((rows, qw - wide), jnp.float32)], axis=1)
            shift = (h * HEAD_DIM - g * HEAD_DIM) % qw
            total = total + (o if shift == 0 else pltpu.roll(o, shift, 1))
        att_ref[...] = total.astype(jnp.bfloat16)


def attention(slot, scal, own, other, gain, wq, wk, wv, cos, sin, keys, values):
    half, width = own.shape
    rows = 2 * half
    qw, kw = wq.shape[1], wk.shape[1]
    heads, kv_heads = qw // HEAD_DIM, kw // HEAD_DIM
    window = keys.shape[1]
    wide = -(-(kw + 1) // 128) * 128
    whole = lambda a: pl.BlockSpec(a.shape, lambda i, s: (0,) * a.ndim)
    of_slot = lambda a: pl.BlockSpec(
        (None,) + a.shape[1:], lambda i, s: (slot,) + (0,) * (a.ndim - 1)
    )
    out = lambda w: (jax.ShapeDtypeStruct((rows, w), jnp.bfloat16))
    return pl.pallas_call(
        functools.partial(attention_kernel, kv_heads, heads // kv_heads),
        grid_spec=pltpu.PrefetchScalarGridSpec(
            num_scalar_prefetch=1,
            grid=(1,),
            in_specs=[
                whole(own),
                whole(other),
                whole(gain),
                whole(wq),
                whole(wk),
                whole(wv),
                of_slot(cos),
                of_slot(sin),
                of_slot(keys),
                of_slot(values),
            ],
            out_specs=[
                pl.BlockSpec((rows, w), lambda i, s: (0, 0)) for w in (qw, kw, kw)
            ],
            scratch_shapes=[
                pltpu.VMEM((rows, width), jnp.bfloat16),
                pltpu.VMEM((heads, rows, kw), jnp.bfloat16),
                pltpu.VMEM((rows, kw), jnp.bfloat16),
                pltpu.VMEM((rows, wide), jnp.float32),
                pltpu.VMEM((window + rows, wide), jnp.bfloat16),
                pltpu.VMEM((heads, rows, wide), jnp.float32),
                pltpu.VMEM((heads, rows, 128), jnp.float32),
            ],
        ),
        out_shape=[out(qw), out(kw), out(kw)],
        compiler_params=pltpu.CompilerParams(vmem_limit_bytes=48 * 1024 * 1024),
        cost_estimate=pl.CostEstimate(
            flops=12 * 10**9, bytes_accessed=12 * 10**6, transcendentals=9 * 10**6
        ),
        name="attention",
    )(scal, own, other, gain, wq, wk, wv, cos, sin, keys, values)


def local(
    hidden_in,
    cache_keys,
    stored_cache_values,
    cache_lengths,
    live_slots,
    attn_gain,
    w_query,
    key_weight,
    value_weight,
    w_out,
    mlp_gain,
    w_gate,
    w_up,
    w_down,
):
    slots, half, width = hidden_in.shape
    rows = 2 * half
    qw = w_query.shape[1]
    tok = lax.axis_index("tok")
    req = lax.axis_index("req")
    reqs = lax.axis_size("req")
    swap = [(0, 1), (1, 0)]
    other_half = lambda a: lax.ppermute(a, "tok", swap)

    others = [other_half(hidden_in[s]) for s in range(slots)]
    share = w_out.shape[0] // reqs
    piece = lax.dynamic_slice_in_dim(w_out, req * share, share, 0)
    w_other = lax.all_gather(other_half(piece), "req", axis=0, tiled=True)

    alive = lax.dynamic_slice_in_dim(live_slots, req * slots, slots)
    index = jnp.arange(rows, dtype=jnp.int32)
    token = index + jnp.where(index < half, tok * half, -tok * half)
    positions = cache_lengths[:, None] + token[None, :]
    h2 = HEAD_DIM // 2
    inverse = ROPE_BASE ** (-(jnp.arange(h2, dtype=jnp.float32) * 2.0) / HEAD_DIM)
    angles = positions.astype(jnp.float32)[..., None] * inverse
    c, s_ = jnp.cos(angles), jnp.sin(angles)
    cos = jnp.tile(jnp.concatenate([c, c], axis=-1), (1, 1, qw // HEAD_DIM))
    sin = jnp.tile(jnp.concatenate([-s_, s_], axis=-1), (1, 1, qw // HEAD_DIM))

    attended = []
    new_keys = []
    new_values = []
    for s in range(slots):
        scal = jnp.stack([cache_lengths[s], alive[s], tok.astype(jnp.int32)])
        a, k, v = attention(
            s,
            scal,
            hidden_in[s],
            others[s],
            attn_gain[None, :],
            w_query,
            key_weight,
            value_weight,
            cos,
            sin,
            cache_keys,
            stored_cache_values,
        )
        attended.append(a)
        new_keys.append(k)
        new_values.append(v)
    results = []
    for s in range(slots):
        a = attended[s]
        b = other_half(a)
        b = jnp.concatenate([b[half:], b[:half]], axis=0)
        hid = jnp.concatenate([hidden_in[s], others[s]], axis=0).astype(jnp.float32)
        residual = (
            hid
            + jnp.dot(a, w_out, preferred_element_type=jnp.float32)
            + jnp.dot(b, w_other, preferred_element_type=jnp.float32)
        ).astype(jnp.bfloat16)
        wide = residual.astype(jnp.float32)
        ms = jnp.mean(wide * wide, axis=-1, keepdims=True)
        mlp_in = (wide * lax.rsqrt(ms + EPSILON) * mlp_gain).astype(jnp.bfloat16)
        gate = jnp.dot(mlp_in, w_gate, preferred_element_type=jnp.float32)
        up = jnp.dot(mlp_in, w_up, preferred_element_type=jnp.float32)
        act = (jax.nn.silu(gate) * up).astype(jnp.bfloat16)
        sent = other_half(
            jnp.dot(act[half:], w_down, preferred_element_type=jnp.float32).astype(jnp.bfloat16)
        )
        mine = jnp.dot(act[:half], w_down, preferred_element_type=jnp.float32)
        out = wide[:half] + mine + sent.astype(jnp.float32)
        out = jnp.where(alive[s] > 0, out, 0.0).astype(jnp.bfloat16)
        results.append(out)
    return (jnp.stack(results), jnp.stack(new_keys), jnp.stack(new_values))


def solution(mesh):
    return jax.shard_map(
        local,
        mesh=mesh,
        in_specs=(
            P("req", "tok", None),
            P("req", None, "tok"),
            P("req", None, "tok"),
            P("req"),
            P(),
            P(),
            P(None, "tok"),
            P(None, "tok"),
            P(None, "tok"),
            P("tok", None),
            P(),
            P(None, "tok"),
            P(None, "tok"),
            P("tok", None),
        ),
        out_specs=(P("req", "tok", None), P("req", None, "tok"), P("req", None, "tok")),
        check_vma=False,
    )
```

time: 789 us -> 165 us (0.21)
  the two profiles are of different devices: /device:TPU:1 before, /device:TPU:17 now
where the time goes in v1:
time: 165 us; the launch traced here: 168 us
  local copies, waits for them, and re-layouts  39.7 us (24%)
  matrix products  38.2 us (23%)
  Pallas kernels  37.4 us (23%)
  waiting for transfers between devices  24.5 us (15%)
  between operations  15.8 us (10%)
  starting transfers between devices  6.81 us (4%)
  other arithmetic  5.21 us (3%)
    pallas_call x2, Pallas kernels, attention(): pl.pallas_call(functools.partial(attention_kernel, kv_heads, heads // kv_...  37.4 us
    unnamed x62, local copies, waits for them, and re-layouts  25.8 us
    ppermute x7, waiting for transfers between devices, local(): other_half = lambda a: lax.ppermute(a, 'tok', swap)  24.5 us
    dot_general x2, matrix products, local(): up = jnp.dot(mlp_in, w_up, preferred_element_type=jnp.float32)  9.41 us
    dot_general x2, matrix products, local(): gate = jnp.dot(mlp_in, w_gate, preferred_element_type=jnp.float32)  8.95 us
    dot_general x2, matrix products, local(): jnp.dot(b, w_other, preferred_element_type=jnp.float32)  7.92 us
    ppermute x7, starting transfers between devices, local(): other_half = lambda a: lax.ppermute(a, 'tok', swap)  6.77 us
    dot_general x2, matrix products, local(): jnp.dot(a, w_out, preferred_element_type=jnp.float32)  6.38 us
  transfers between devices with their start and end apart: 8, of which 4 were waited for; matrix products, arithmetic and copies ran while one was open for 35% of the time, Pallas kernels for 22%

profile of v1, /device:TPU:17, one launch (start us, length us, event | category | flops | bytes accessed | tf_op | source)
XLA Modules:
  0.0 167.6 jit_solution(5863312714141567650)
XLA Ops:
  7.3 1.8 %copy-done = bf16[640,2560]{1,0:T(8,128)(2,1)S(1)} copy-done((bf16[640,2560]{1,0:T(8,128)(2,1)S(1)}, bf16[640,2560]{1,0:T(8,128)(2,1)}, u32[]{:S(2)}) %copy-start) | copy-done | bytes 3276824
  9.1 1.3 collective-permute-start.2
  10.4 4.7 %collective-permute-done.2 = bf16[40,2560]{1,0:T(8,128)(2,1)S(1)} collective-permute-done((bf16[40,2560]{1,0:T(8,128)(2,1)S(1)}, bf16[40,2560]{1,0:T(8,128)(2,1)S(1)}, u32[]{:S(2)}, u32[]{:S(2)}) %collective-permute-start.2) | collective-permute-done | bytes 204832 | tf_op jit(solution)/shard_map/ppermute | solution.py:241
  15.1 0.7 copy-done.14
  15.8 2.4 %slice_bitcast_fusion.1 = (bf16[128,2560]{1,0:T(8,128)(2,1)}, bf16[128,2560]{1,0:T(8,128)(2,1)}) fusion(bf16[2,128,2560]{2,1,0:T(8,128)(2,1)} %param.14), kind=kLoop, calls=%fused_computation.26 | loop fusion | bytes 2621440 | tf_op jit(solution)/shard_map/squeeze | solution.py:286
  18.3 1.2 collective-permute-start
  19.8 0.6 fusion.36
  21.9 0.4 fusion.28
  22.3 1.2 tile.8
  23.5 2.8 %copy.29.cos_ref = f32[2,256,640]{2,1,0:T(8,128)} copy(f32[2,256,640]{1,2,0:T(8,128)} %bitcast.37) | data formatting | bytes 2621440 | tf_op jit(solution)/shard_map/tile | solution.py:256
  26.3 2.3 %copy.27.wk_ref = bf16[2560,160]{1,0:T(8,128)(2,1)} copy(bf16[2560,160]{0,1:T(8,128)(2,1)} %param.21) | data formatting | bytes 1638400 | tf_op args[7]
  28.6 2.4 %copy.28.wv_ref = bf16[2560,160]{1,0:T(8,128)(2,1)} copy(bf16[2560,160]{0,1:T(8,128)(2,1)} %param.22) | data formatting | bytes 1638400 | tf_op args[8]
  31.0 1.2 tile.20
  32.2 2.8 %copy.30.sin_ref = f32[2,256,640]{2,1,0:T(8,128)} copy(f32[2,256,640]{1,2,0:T(8,128)} %bitcast.38) | data formatting | bytes 2621440 | tf_op jit(solution)/shard_map/tile | solution.py:257
  35.0 5.5 %copy.31.k_ref = bf16[2,4096,160]{2,1,0:T(8,128)(2,1)} copy(bf16[2,4096,160]{1,2,0:T(8,128)(2,1)} %param.15) | data formatting | bytes 5242880 | tf_op args[1]
  40.6 5.6 %copy.32.v_ref = bf16[2,4096,160]{2,1,0:T(8,128)(2,1)} copy(bf16[2,4096,160]{1,2,0:T(8,128)(2,1)} %param.16) | data formatting | bytes 5242880 | tf_op args[2]
  46.2 1.3 add_add_fusion.scal_ref
  47.5 1.4 add_add_fusion.1.scal_ref
  48.9 1.4 copy-done.2
  50.3 1.3 copy-done.4
  51.6 1.3 copy-done.6
  52.9 13.4 %attention.3 = (bf16[256,640]{1,0:T(8,128)(2,1)S(1)}, bf16[256,160]{1,0:T(8,128)(2,1)S(1)}, bf16[256,160]{1,0:T(8,128)(2,1)S(1)}) custom-call(s32[3]{0:T(128)S(1)} %add_add_fusion.1.scal_ref, bf16[128,2560]{1,0:T(8,128)(2,1)} %get-tuple-element.22.own_ref, bf16[128,2560]{1,0:T(8,128)(2,1)} %collective-permute-done.4.other_ref, ...), custom_call_target="tpu_custom_call" | custom-call | flops 12000000000 | bytes 12000000 | tf_op jit(solution)/shard_map/attention/pallas_call | solution.py:179
  66.3 24.1 %attention.2 = (bf16[256,640]{1,0:T(8,128)(2,1)S(1)}, bf16[256,160]{1,0:T(8,128)(2,1)S(1)}, bf16[256,160]{1,0:T(8,128)(2,1)S(1)}) custom-call(s32[3]{0:T(128)S(1)} %add_add_fusion.scal_ref, bf16[128,2560]{1,0:T(8,128)(2,1)} %get-tuple-element.21.own_ref, bf16[128,2560]{1,0:T(8,128)(2,1)} %collective-permute-done.other_ref, ...), custom_call_target="tpu_custom_call" | custom-call | flops 12000000000 | bytes 12000000 | tf_op jit(solution)/shard_map/attention/pallas_call | solution.py:179
  90.4 0.7 copy-done.9
  91.1 0.8 pad_maximum_fusion.1
  91.9 1.8 %copy.39 = bf16[2,256,160]{1,2,0:T(8,128)(2,1)} copy(bf16[2,256,160]{2,1,0:T(8,128)(2,1)} %pad_maximum_fusion.1) | data formatting | bytes 327680
  93.7 1.2 collective-permute-start.5
  95.1 3.7 %fusion.39 = f32[256,2560]{1,0:T(8,128)} fusion(bf16[256,640]{1,0:T(8,128)(2,1)} %copy-done.8, bf16[640,2560]{1,0:T(8,128)(2,1)S(1)} %copy-done), kind=kOutput, calls=%fused_computation.64 | convolution fusion | flops 838860800 | bytes 6225920 | tf_op jit(solution)/shard_map/dot_general | solution.py:289
  98.8 2.7 %fusion.38 = f32[256,2560]{1,0:T(8,128)} fusion(bf16[256,640]{1,0:T(8,128)(2,1)S(1)} %copy-done.10, bf16[640,2560]{1,0:T(8,128)(2,1)S(1)} %copy-done), kind=kOutput, calls=%fused_computation.63 | convolution fusion | flops 838860800 | bytes 6225920 | tf_op jit(solution)/shard_map/dot_general | solution.py:289
  101.6 0.8 copy.40
  102.4 1.3 collective-permute-done.5
  103.7 1.0 fusion.35
  104.7 4.6 %collective-permute-done.1 = bf16[256,640]{1,0:T(8,128)(2,1)} collective-permute-done((bf16[256,640]{1,0:T(8,128)(2,1)}, bf16[256,640]{1,0:T(8,128)(2,1)}, u32[]{:S(2)}, u32[]{:S(2)}) %collective-permute-start.1) | collective-permute-done | bytes 327712 | tf_op jit(solution)/shard_map/ppermute | solution.py:241
  109.4 1.7 %fusion.34 = (bf16[128,640]{1,0:T(8,128)(2,1)S(1)}, bf16[128,640]{1,0:T(8,128)(2,1)}) fusion(bf16[256,640]{1,0:T(8,128)(2,1)} %collective-permute-done.1), kind=kLoop, calls=%fused_computation.59 | loop fusion | bytes 655360 | tf_op jit(solution)/shard_map/slice | solution.py:285
  111.1 4.5 %multiply_reduce_fusion = (f32[256]{0:T(256)S(1)}, f32[256,2560]{1,0:T(8,128)S(1)}) fusion(bf16[640,2560]{1,0:T(8,128)(2,1)} %all-gather.2.cloned.1.call-done, bf16[128,640]{1,0:T(8,128)(2,1)S(1)} %get-tuple-element.26, bf16[128,640]{1,0:T(8,128)(2,1)S(1)} %get-tuple-element.25, f32[256,2560]{1,0:T(8,128)} %fusion.39, ...), kind=kOutput, calls=%fused_computation.7 | convolution fusion | flops 846069504 | bytes 10159104 | tf_op jit(solution)/shard_map/dot_general | solution.py:290
  115.6 6.3 %fusion.33 = f32[256,1792]{1,0:T(8,128)S(1)} fusion(bf16[2560,1792]{1,0:T(8,128)(2,1)} %param.25, f32[256,2560]{1,0:T(8,128)S(1)} %get-tuple-element.35, f32[256]{0:T(256)S(1)} %add_rsqrt_fusion, f32[2560]{0:T(1024)S(1)} %copy-done.17), kind=kOutput, calls=%fused_computation.58 | convolution fusion | flops 2350776320 | bytes 13642752 | tf_op jit(solution)/shard_map/dot_general | solution.py:295
  122.0 2.8 %fusion.1 = bf16[256,1792]{1,0:T(8,128)(2,1)S(1)} fusion(bf16[2560,1792]{1,0:T(8,128)(2,1)S(1)} %bitcast.42, f32[256,1792]{1,0:T(8,128)S(1)} %fusion.33, f32[256,2560]{1,0:T(8,128)S(1)} %get-tuple-element.35, f32[256]{0:T(256)S(1)} %add_rsqrt_fusion, f32[2560]{0:T(1024)S(1)} %copy-done.17), kind=kOutput, calls=%fused_computation.13 | convolution fusion | flops 2353528832 | bytes 14560256 | tf_op jit(solution)/shard_map/dot_general | solution.py:296
  124.9 1.4 convolution_convert_fusion
  126.2 1.3 collective-permute-start.6
  127.5 3.5 %multiply_reduce_fusion.1 = (f32[256]{0:T(256)S(1)}, f32[256,2560]{1,0:T(8,128)S(1)}) fusion(bf16[640,2560]{1,0:T(8,128)(2,1)S(1)} %copy-done.11, bf16[128,640]{1,0:T(8,128)(2,1)S(1)} %copy-done.13, bf16[128,640]{1,0:T(8,128)(2,1)S(1)} %get-tuple-element.23, f32[256,2560]{1,0:T(8,128)S(1)} %copy-done.12, ...), kind=kOutput, calls=%fused_computation.10 | convolution fusion | flops 846069504 | bytes 10159104 | tf_op jit(solution)/shard_map/dot_general | solution.py:290
  131.0 2.6 %fusion.32 = f32[256,1792]{1,0:T(8,128)S(1)} fusion(bf16[2560,1792]{1,0:T(8,128)(2,1)S(1)} %bitcast.40, f32[256,2560]{1,0:T(8,128)S(1)} %get-tuple-element.37, f32[2560]{0:T(1024)S(1)} %copy-done.17, f32[256]{0:T(256)S(1)} %add_rsqrt_fusion.1), kind=kOutput, calls=%fused_computation.57 | convolution fusion | flops 2350776320 | bytes 13642752 | tf_op jit(solution)/shard_map/dot_general | solution.py:295
  133.7 6.6 %fusion = bf16[256,1792]{1,0:T(8,128)(2,1)S(1)} fusion(bf16[2560,1792]{1,0:T(8,128)(2,1)} %param.26, f32[256,1792]{1,0:T(8,128)S(1)} %fusion.32, f32[256,2560]{1,0:T(8,128)S(1)} %get-tuple-element.37, f32[2560]{0:T(1024)S(1)} %copy-done.17, f32[256]{0:T(256)S(1)} %add_rsqrt_fusion.1), kind=kOutput, calls=%fused_computation.12 | convolution fusion | flops 2353528832 | bytes 14560256 | tf_op jit(solution)/shard_map/dot_general | solution.py:296
  140.3 1.4 convolution_convert_fusion.1
  141.7 1.3 collective-permute-start.3
  143.0 1.5 fusion.7
  144.4 13.8 %collective-permute-done.3 = bf16[128,2560]{1,0:T(8,128)(2,1)S(1)} collective-permute-done((bf16[128,2560]{1,0:T(8,128)(2,1)S(1)}, bf16[128,2560]{1,0:T(8,128)(2,1)S(1)}, u32[]{:S(2)}, u32[]{:S(2)}) %collective-permute-start.3) | collective-permute-done | bytes 655392 | tf_op jit(solution)/shard_map/ppermute | solution.py:241
  158.2 1.4 fusion.11
  159.6 1.2 pad_maximum_fusion
  (71 shorter events, 1.0 us)
Async XLA Ops:
  7.2 1.9 %copy-start = (bf16[640,2560]{1,0:T(8,128)(2,1)S(1)}, bf16[640,2560]{1,0:T(8,128)(2,1)}, u32[]{:S(2)}) copy-start(bf16[640,2560]{1,0:T(8,128)(2,1)} %param.23) | copy-start | bytes 9830404
  7.2 12.6 %copy-start.18 = (s32[32]{0:T(128)S(1)}, s32[32]{0:T(128)}, u32[]{:S(2)}) copy-start(s32[32]{0:T(128)} %param.18) | copy-start | bytes 388
  7.2 12.6 %copy-start.16 = (s32[2]{0:T(128)S(1)}, s32[2]{0:T(128)}, u32[]{:S(2)}) copy-start(s32[2]{0:T(128)} %param.17) | copy-start | bytes 28
  7.2 14.6 %copy-start.15 = (f32[2560]{0:T(1024)S(1)}, f32[2560]{0:T(1024)}, u32[]{:S(2)}) copy-start(f32[2560]{0:T(1024)} %param.19) | copy-start | bytes 30724
  7.2 103.8 %all-gather.2.cloned.1.call-start = ((), (), s32[]{:S(2)}) async-start(), calls=%async_computation | async-start | bytes 3481600 | tf_op jit(solution)/shard_map/all_gather | solution.py:246
  9.1 6.0 %collective-permute-start.2 = (bf16[40,2560]{1,0:T(8,128)(2,1)S(1)}, bf16[40,2560]{1,0:T(8,128)(2,1)S(1)}, u32[]{:S(2)}, u32[]{:S(2)}) collective-permute-start(bf16[40,2560]{1,0:T(8,128)(2,1)S(1)} %constant_dynamic-slice_fusion), channel_id=1, source_target_pairs={{0,1},{1,0},{2,3},{3,2},{4,5},{5,4},{6,7},{7,6},{8,9},{9,8},{10,11... | collective-permute-start | bytes 614408 | tf_op jit(solution)/shard_map/ppermute | solution.py:241
  15.1 0.7 copy-start.14
  18.3 48.0 %collective-permute-start = (bf16[128,2560]{1,0:T(8,128)(2,1)}, bf16[128,2560]{1,0:T(8,128)(2,1)}, u32[]{:S(2)}, u32[]{:S(2)}) collective-permute-start(bf16[128,2560]{1,0:T(8,128)(2,1)} %get-tuple-element.21.own_ref), channel_id=1, source_target_pairs={{0,1},{1,0},{2,3},{3,2},{4,5},{5,4},{6,7},{7,6},{8,9},{9,8},{10,11... | collective-permute-start | bytes 1966088 | tf_op jit(solution)/shard_map/ppermute | solution.py:241
  19.5 29.4 %collective-permute-start.4 = (bf16[128,2560]{1,0:T(8,128)(2,1)}, bf16[128,2560]{1,0:T(8,128)(2,1)}, u32[]{:S(2)}, u32[]{:S(2)}) collective-permute-start(bf16[128,2560]{1,0:T(8,128)(2,1)} %get-tuple-element.22.own_ref), channel_id=1, source_target_pairs={{0,1},{1,0},{2,3},{3,2},{4,5},{5,4},{6,7},{7,6},{8,9},{9,8},{10,11... | collective-permute-start | bytes 1966088 | tf_op jit(solution)/shard_map/ppermute | solution.py:241
  48.9 1.4 copy-start.2
  50.3 1.3 copy-start.4
  51.6 1.3 copy-start.6
  52.9 13.4 %copy-start.3 = (f32[2,256,640]{2,1,0:T(8,128)S(1)}, f32[2,256,640]{2,1,0:T(8,128)}, u32[]{:S(2)}) copy-start(f32[2,256,640]{2,1,0:T(8,128)} %copy.29.cos_ref) | copy-start | bytes 3932164
  52.9 13.4 %copy-start.5 = (bf16[2560,160]{1,0:T(8,128)(2,1)S(1)}, bf16[2560,160]{1,0:T(8,128)(2,1)}, u32[]{:S(2)}) copy-start(bf16[2560,160]{1,0:T(8,128)(2,1)} %copy.27.wk_ref) | copy-start | bytes 2457604
  52.9 13.4 %copy-start.7 = (bf16[2560,160]{1,0:T(8,128)(2,1)S(1)}, bf16[2560,160]{1,0:T(8,128)(2,1)}, u32[]{:S(2)}) copy-start(bf16[2560,160]{1,0:T(8,128)(2,1)} %copy.28.wv_ref) | copy-start | bytes 2457604
  66.3 24.1 %copy-start.8 = (bf16[256,640]{1,0:T(8,128)(2,1)}, bf16[256,640]{1,0:T(8,128)(2,1)S(1)}, u32[]{:S(2)}) copy-start(bf16[256,640]{1,0:T(8,128)(2,1)S(1)} %get-tuple-element.10) | copy-start | bytes 983044
  90.4 0.7 copy-start.9
  93.7 10.0 %collective-permute-start.5 = (bf16[256,640]{1,0:T(8,128)(2,1)}, bf16[256,640]{1,0:T(8,128)(2,1)}, u32[]{:S(2)}, u32[]{:S(2)}) collective-permute-start(bf16[256,640]{1,0:T(8,128)(2,1)} %copy-done.8), channel_id=1, source_target_pairs={{0,1},{1,0},{2,3},{3,2},{4,5},{5,4},{6,7},{7,6},{8,9},{9,8},{10,11... | collective-permute-start | bytes 983048 | tf_op jit(solution)/shard_map/ppermute | solution.py:241
  94.9 3.9 %copy-start.10 = (bf16[256,640]{1,0:T(8,128)(2,1)S(1)}, bf16[256,640]{1,0:T(8,128)(2,1)}, u32[]{:S(2)}) copy-start(bf16[256,640]{1,0:T(8,128)(2,1)} %copy-done.9) | copy-start | bytes 983044
  94.9 14.5 %collective-permute-start.1 = (bf16[256,640]{1,0:T(8,128)(2,1)}, bf16[256,640]{1,0:T(8,128)(2,1)}, u32[]{:S(2)}, u32[]{:S(2)}) collective-permute-start(bf16[256,640]{1,0:T(8,128)(2,1)} %copy-done.9), channel_id=1, source_target_pairs={{0,1},{1,0},{2,3},{3,2},{4,5},{5,4},{6,7},{7,6},{8,9},{9,8},{10,11... | collective-permute-start | bytes 983048 | tf_op jit(solution)/shard_map/ppermute | solution.py:241
  111.1 4.5 %copy-start.17 = (f32[2560]{0:T(1024)S(1)}, f32[2560]{0:T(1024)}, u32[]{:S(2)}) copy-start(f32[2560]{0:T(1024)} %param.24) | copy-start | bytes 30724
  111.1 10.9 %slice-start.6 = ((s8[9175040]{0:T(1024)(128)(4,1)}), s8[4194304]{0:T(1024)(128)(4,1)S(1)}, s32[]{:S(2)}) async-start(s8[9175040]{0:T(1024)(128)(4,1)} %bitcast.41), calls=%async_computation.7 | async-start | bytes 8388608
  115.5 6.4 %slice-start.7 = ((s8[9175040]{0:T(1024)(128)(4,1)}), s8[4194304]{0:T(1024)(128)(4,1)S(1)}, s32[]{:S(2)}) async-start(s8[9175040]{0:T(1024)(128)(4,1)} %bitcast.41), calls=%async_computation.8 | async-start | bytes 8388608
  115.6 6.4 %slice-start.8 = ((s8[9175040]{0:T(1024)(128)(4,1)}), s8[786432]{0:T(1024)(128)(4,1)S(1)}, s32[]{:S(2)}) async-start(s8[9175040]{0:T(1024)(128)(4,1)} %bitcast.41), calls=%async_computation.9 | async-start | bytes 1572864
  115.6 9.2 %slice-start = ((s8[9175040]{0:T(1024)(128)(4,1)}), s8[4194304]{0:T(1024)(128)(4,1)S(1)}, s32[]{:S(2)}) async-start(s8[9175040]{0:T(1024)(128)(4,1)} %bitcast.35), calls=%async_computation.1 | async-start | bytes 8388608
  115.6 9.2 %slice-start.1 = ((s8[9175040]{0:T(1024)(128)(4,1)}), s8[4194304]{0:T(1024)(128)(4,1)S(1)}, s32[]{:S(2)}) async-start(s8[9175040]{0:T(1024)(128)(4,1)} %bitcast.35), calls=%async_computation.2 | async-start | bytes 8388608
  122.0 2.8 %slice-start.2 = ((s8[9175040]{0:T(1024)(128)(4,1)}), s8[786432]{0:T(1024)(128)(4,1)S(1)}, s32[]{:S(2)}) async-start(s8[9175040]{0:T(1024)(128)(4,1)} %bitcast.35), calls=%async_computation.3 | async-start | bytes 1572864
  124.8 2.7 %copy-start.11 = (bf16[640,2560]{1,0:T(8,128)(2,1)S(1)}, bf16[640,2560]{1,0:T(8,128)(2,1)}, u32[]{:S(2)}) copy-start(bf16[640,2560]{1,0:T(8,128)(2,1)} %all-gather.2.cloned.1.call-done) | copy-start | bytes 9830404
  124.8 2.7 %copy-start.12 = (f32[256,2560]{1,0:T(8,128)S(1)}, f32[256,2560]{1,0:T(8,128)}, u32[]{:S(2)}) copy-start(f32[256,2560]{1,0:T(8,128)} %fusion.38) | copy-start | bytes 7864324
  124.8 2.7 %copy-start.13 = (bf16[128,640]{1,0:T(8,128)(2,1)S(1)}, bf16[128,640]{1,0:T(8,128)(2,1)}, u32[]{:S(2)}) copy-start(bf16[128,640]{1,0:T(8,128)(2,1)} %get-tuple-element.24) | copy-start | bytes 491524
  124.8 6.2 %slice-start.3 = ((s8[9175040]{0:T(1024)(128)(4,1)}), s8[4194304]{0:T(1024)(128)(4,1)S(1)}, s32[]{:S(2)}) async-start(s8[9175040]{0:T(1024)(128)(4,1)} %bitcast.39), calls=%async_computation.4 | async-start | bytes 8388608
  124.8 6.2 %slice-start.4 = ((s8[9175040]{0:T(1024)(128)(4,1)}), s8[4194304]{0:T(1024)(128)(4,1)S(1)}, s32[]{:S(2)}) async-start(s8[9175040]{0:T(1024)(128)(4,1)} %bitcast.39), calls=%async_computation.5 | async-start | bytes 8388608
  126.2 16.7 %collective-permute-start.6 = (bf16[128,2560]{1,0:T(8,128)(2,1)S(1)}, bf16[128,2560]{1,0:T(8,128)(2,1)S(1)}, u32[]{:S(2)}, u32[]{:S(2)}) collective-permute-start(bf16[128,2560]{1,0:T(8,128)(2,1)S(1)} %convolution_convert_fusion), channel_id=1, source_target_pairs={{0,1},{1,0},{2,3},{3,2},{4,5},{5,4},{6,7},{7,6},{8,9},{9,8},{10,11... | collective-permute-start | bytes 1966088 | tf_op jit(solution)/shard_map/ppermute | solution.py:241
  127.5 3.5 %slice-start.5 = ((s8[9175040]{0:T(1024)(128)(4,1)}), s8[786432]{0:T(1024)(128)(4,1)S(1)}, s32[]{:S(2)}) async-start(s8[9175040]{0:T(1024)(128)(4,1)} %bitcast.39), calls=%async_computation.6 | async-start | bytes 1572864
  141.7 16.5 %collective-permute-start.3 = (bf16[128,2560]{1,0:T(8,128)(2,1)S(1)}, bf16[128,2560]{1,0:T(8,128)(2,1)S(1)}, u32[]{:S(2)}, u32[]{:S(2)}) collective-permute-start(bf16[128,2560]{1,0:T(8,128)(2,1)S(1)} %convolution_convert_fusion.1), channel_id=1, source_target_pairs={{0,1},{1,0},{2,3},{3,2},{4,5},{5,4},{6,7},{7,6},{8,9},{9,8},{10,11... | collective-permute-start | bytes 1966088 | tf_op jit(solution)/shard_map/ppermute | solution.py:241
  158.2 2.6 %copy-start.1 = (bf16[640,2560]{1,0:T(8,128)(2,1)S(1)}, bf16[640,2560]{1,0:T(8,128)(2,1)}, u32[]{:S(2)}) copy-start(bf16[640,2560]{1,0:T(8,128)(2,1)} %param.23) | copy-start | bytes 9830404
Sparse Core Ops, SparseCore 0:
  16.0 48.1 all-gather.1
